TPU v7x, 32 devices: a whole 2x2x4 slice. The times are simulated.
32 devices in a mesh: scale: 8 (over y, x, core), rt: 4 (over z).
Axes of the slice: x: 2, y: 2, z: 4, core: 2. Of those that a mesh axis runs over, the one named last changes fastest.
Arguments:
- slab: float32 [96, 128, 896], P('rt'), may hold values from -6 to 6
- widths: int32 [8], replicated, may hold values from 1 to 8
Outputs:
- peak: bfloat16 [96, 128, 896], P('rt', 'scale')
- energy: float32 [96, 128, 896], P('rt', 'scale')
All inputs are finite; a program needn't handle non-finite values.
Results may differ from a plain program's by a relative error of at most 0.006.
Values may be sent and summed in bfloat16 or wider, within the bound.
A program may use at most 128 MiB of HBM per device.

v0:
```python
import jax
import jax.numpy as jnp
from jax import lax
from jax.sharding import PartitionSpec as P

SC_DEV = 1
SCAN_RATIO = 16


def padded_2(block, sides, width):
    for axis, dim in sides:
        count = lax.axis_size(axis)
        forward = [(i, i + 1) for i in range(count - 1)]
        backward = [(target, source) for source, target in forward]
        low = lax.ppermute(
            lax.slice_in_dim(block, block.shape[dim] - width, None, axis=dim), axis, forward
        )
        high = lax.ppermute(lax.slice_in_dim(block, 0, width, axis=dim), axis, backward)
        block = jnp.concatenate([low, block, high], axis=dim)
    return block


def mexican(offsets, spread):
    ratio = offsets / spread
    return (1.0 - ratio * ratio) * jnp.exp(-0.5 * ratio * ratio) / jnp.sqrt(spread)


def scan_offsets(scan_count):
    positions = jnp.arange(scan_count, dtype=jnp.float32)
    return positions[:, None] - positions[None, :]


def frame_table(frame_rows, scale_width):
    out_pos = jnp.arange(frame_rows, dtype=jnp.float32)
    in_pos = jnp.arange(3 * frame_rows, dtype=jnp.float32)
    offsets = in_pos[None, :] - frame_rows - out_pos[:, None]
    values = jnp.where(jnp.abs(offsets) <= frame_rows, mexican(offsets, scale_width), 0.0)
    return values.astype(jnp.bfloat16)


def per_device(slab, widths):
    frame_rows, mz_bins, scan_count = slab.shape
    scan_diff = scan_offsets(scan_count)
    signal = slab.astype(jnp.bfloat16).reshape(frame_rows * mz_bins, scan_count)
    first_scale = lax.axis_index("scale") * SC_DEV
    scale_width = lax.dynamic_slice_in_dim(widths, first_scale + 0, 1)[0].astype(jnp.float32)
    scan_table = mexican(scan_diff, SCAN_RATIO * scale_width).astype(jnp.bfloat16)
    smooth = jnp.dot(signal, scan_table, preferred_element_type=jnp.float32).astype(jnp.bfloat16)
    smooth = smooth.reshape(frame_rows, mz_bins, scan_count)
    padded = padded_2(smooth, (("rt", 0),), frame_rows)
    answer = jnp.dot(
        frame_table(frame_rows, scale_width),
        padded.reshape(3 * frame_rows, -1),
        preferred_element_type=jnp.float32,
    )
    answers = [answer.astype(jnp.bfloat16).reshape(frame_rows, mz_bins, scan_count)]
    stacked = jnp.stack(answers, axis=0)
    block = lax.all_to_all(stacked, "scale", split_axis=2, concat_axis=0, tiled=True)
    peak = jnp.max(block, axis=0)
    energy = jnp.sum(jnp.square(block.astype(jnp.float32)), axis=0)
    return (peak, energy)


def solution(mesh):
    in_specs = (P("rt", None, None), P())
    out_specs = (P("rt", "scale", None), P("rt", "scale", None))
    return jax.shard_map(
        per_device, mesh=mesh, in_specs=in_specs, out_specs=out_specs, check_vma=False
    )
```

profile of v0, /device:TPU:0, one launch (start us, length us, event | category | flops | bytes accessed | tf_op | source)
XLA Modules:
  0.0 256.3 jit_solution(14131368741015180085)
XLA Ops:
  0.6 1.2 dynamic_slice.3
  2.6 5.0 %convert_element_type.32 = bf16[24,128,896]{2,1,0:T(8,128)(2,1)S(1)} convert(f32[24,128,896]{2,1,0:T(8,128)} %param.2) | non-fusion elementwise | flops 2752512 | bytes 16515072 | tf_op jit(solution)/shard_map/convert_element_type | solution.py:44
  7.6 9.0 %convert_bitcast_fusion = bf16[3072,896]{0,1:T(8,128)(2,1)} fusion(bf16[3072,896]{1,0:T(8,128)(2,1)S(1)} %bitcast.24, f32[]{:T(128)S(6)} %sqrt.7, f32[]{:T(128)S(6)} %mul_shard_map.3), kind=kOutput, calls=%fused_computation.7 | convolution fusion | flops 4942479360 | bytes 11010056 | tf_op jit(solution)/shard_map/dot_general | solution.py:48
  16.7 8.0 %copy.17 = bf16[3072,896]{1,0:T(8,128)(2,1)} copy(bf16[3072,896]{0,1:T(8,128)(2,1)} %convert_bitcast_fusion) | data formatting | bytes 11010048 | tf_op jit(solution)/shard_map/reshape | solution.py:49
  24.7 1.3 collective-permute-start.1
  26.0 8.0 %collective-permute-start = (bf16[24,128,896]{2,1,0:T(8,128)(2,1)}, bf16[24,128,896]{2,1,0:T(8,128)(2,1)}, u32[]{:S(2)}, u32[]{:S(2)}) collective-permute-start(bf16[24,128,896]{2,1,0:T(8,128)(2,1)} %bitcast.19), channel_id=1, source_target_pairs={{0,1},{1,2},{2,3},{4,5},{5,6},{6,7},{8,9},{9,10},{10,11},{12,13},{... | collective-permute-start | bytes 16515080 | tf_op jit(solution)/shard_map/ppermute | solution.py:15
  33.9 7.2 %concatenate.11 = bf16[24,114688]{1,0:T(8,128)(2,1)} reshape(bf16[3072,896]{1,0:T(8,128)(2,1)} %copy.17) | data formatting | bytes 11010048 | tf_op jit(solution)/shard_map/concatenate | solution.py:19
  41.2 107.3 %collective-permute-done.1 = bf16[24,128,896]{2,1,0:T(8,128)(2,1)} collective-permute-done((bf16[24,128,896]{2,1,0:T(8,128)(2,1)}, bf16[24,128,896]{2,1,0:T(8,128)(2,1)}, u32[]{:S(2)}, u32[]{:S(2)}) %collective-permute-start.1) | collective-permute-done | bytes 5505056 | tf_op jit(solution)/shard_map/ppermute | solution.py:18
  148.6 8.2 %copy.19 = bf16[3,8,128,896]{3,1,2,0:T(8,128)(2,1)} copy(bf16[3,8,128,896]{3,2,1,0:T(8,128)(2,1)} %bitcast.9) | data formatting | bytes 11010048
  156.7 0.0 collective-permute-done
  156.7 8.1 %copy.18 = bf16[3,8,128,896]{3,1,2,0:T(8,128)(2,1)} copy(bf16[3,8,128,896]{3,2,1,0:T(8,128)(2,1)} %bitcast.7) | data formatting | bytes 11010048
  164.8 8.8 %convolution_convert_fusion = bf16[24,114688]{1,0:T(8,128)(2,1)} fusion(bf16[24,114688]{1,0:T(8,128)(2,1)} %bitcast.21, bf16[24,114688]{1,0:T(8,128)(2,1)} %concatenate.11, bf16[24,114688]{1,0:T(8,128)(2,1)} %bitcast.22, f32[]{:T(128)S(6)} %sqrt.6, f32[]{:T(128)} %bitcast, f32[72]{0:T(128)S(1)} %iota_add_fusion), kind=kOutput, calls=%fused_computation | convolution fusion | flops 448680192 | bytes 22020392 | tf_op jit(solution)/shard_map/dot_general | solution.py:51
  173.7 3.6 %copy.20 = bf16[3,8,128,896]{3,2,1,0:T(8,128)(2,1)S(1)} copy(bf16[3,8,128,896]{3,1,2,0:T(8,128)(2,1)} %bitcast.23) | data formatting | bytes 11010048
  177.2 3.2 %copy.14 = bf16[1,24,128,896]{3,1,0,2:T(8,128)(2,1)S(1)} copy(bf16[1,24,128,896]{3,2,1,0:T(8,128)(2,1)S(1)} %bitcast.20) | data formatting | bytes 11010048 | tf_op jit(solution)/shard_map/stack;reshape | solution.py:57
  180.4 66.8 %all_to_all.15 = bf16[1,24,128,896]{3,1,0,2:T(8,128)(2,1)S(1)} all-to-all(bf16[1,24,128,896]{3,1,0,2:T(8,128)(2,1)S(1)} %copy.14), channel_id=1, replica_groups=mesh['scale'=8,'rt'=4] {'scale'}, dimensions={2} | all-to-all | bytes 11010048 | tf_op jit(solution)/shard_map/all_to_all | solution.py:58
  247.2 0.0 copy-start
  247.2 2.4 copy-done
  249.6 1.1 multiply_reduce_fusion
  250.7 1.3 copy.16
  252.0 3.3 %reduce_max.9 = bf16[24,16,896]{2,0,1:T(8,128)(2,1)S(1)} reduce(bf16[8,1,24,16,896]{4,2,3,0,1:T(8,128)(2,1)} %bitcast.17, bf16[]{:T(256)} %constant.26.clone.1), dimensions={0,1}, to_apply=%region_0.1 | reduce | flops 2408448 | bytes 6193154 | tf_op jit(solution)/shard_map/reduce_max | solution.py:59
  255.3 0.9 copy.15
  (1 shorter events, 0.0 us)
Async XLA Ops:
  24.7 123.9 %collective-permute-start.1 = (bf16[24,128,896]{2,1,0:T(8,128)(2,1)}, bf16[24,128,896]{2,1,0:T(8,128)(2,1)}, u32[]{:S(2)}, u32[]{:S(2)}) collective-permute-start(bf16[24,128,896]{2,1,0:T(8,128)(2,1)} %bitcast.18), channel_id=1, source_target_pairs={{1,0},{2,1},{3,2},{5,4},{6,5},{7,6},{9,8},{10,9},{11,10},{13,12},{... | collective-permute-start | bytes 16515080 | tf_op jit(solution)/shard_map/ppermute | solution.py:18
  26.0 130.8 %collective-permute-start = (bf16[24,128,896]{2,1,0:T(8,128)(2,1)}, bf16[24,128,896]{2,1,0:T(8,128)(2,1)}, u32[]{:S(2)}, u32[]{:S(2)}) collective-permute-start(bf16[24,128,896]{2,1,0:T(8,128)(2,1)} %bitcast.19), channel_id=1, source_target_pairs={{0,1},{1,2},{2,3},{4,5},{5,6},{6,7},{8,9},{9,10},{10,11},{12,13},{... | collective-permute-start | bytes 16515080 | tf_op jit(solution)/shard_map/ppermute | solution.py:15
  247.2 2.4 copy-start
where the time goes:
time: 257 us; the launch traced here: 256 us
  waiting for transfers between devices  107 us (42%)
  blocking collectives  66.8 us (26%)
  local copies, waits for them, and re-layouts  44.1 us (17%)
  matrix products  17.9 us (7%)
  other arithmetic  9.47 us (4%)
  starting transfers between devices  9.23 us (4%)
    ppermute x1, waiting for transfers between devices, padded_2(): lax.ppermute(lax.slice_in_dim(block, 0, width, axis=dim), axis, backward)  107 us
    all_to_all x1, blocking collectives, per_device(): lax.all_to_all(stacked, 'scale', split_axis=2, concat_axis=0, tiled=True)  66.8 us
    unnamed x7, local copies, waits for them, and re-layouts  24.4 us
    dot_general x1, matrix products, per_device(): jnp.dot(signal, scan_table, preferred_element_type=jnp.float32)  9.05 us
    dot_general x1, matrix products, per_device(): jnp.dot(frame_table(frame_rows, scale_width), padded.reshape(3 * frame_ro...  8.84 us
    reshape x1, local copies, waits for them, and re-layouts, per_device(): smooth = smooth.reshape(frame_rows, mz_bins, scan_count)  8.02 us
    ppermute x1, starting transfers between devices, padded_2(): lax.ppermute(lax.slice_in_dim(block, block.shape[dim] - width, None, axis...  7.95 us
    concatenate x1, local copies, waits for them, and re-layouts, padded_2(): block = jnp.concatenate([low, block, high], axis=dim)  7.23 us
  transfers between devices with their start and end apart: 2, of which 1 were waited for; matrix products, arithmetic and copies ran while one was open for 6% of the time, Pallas kernels for 0%

commit v1 on v0

v1 whole, which is shorter than its diff:
```python
import functools

import jax
import jax.numpy as jnp
from jax import lax
from jax.experimental import pallas as pl
from jax.experimental.pallas import tpu as pltpu
from jax.sharding import PartitionSpec as P

SCAN_RATIO = 16
LANES = 128
GROUPS = 2
MESH = pl.DeviceIdType.MESH


def mexican(ratio, spread):
    square = ratio * ratio
    return (1.0 - square) * jnp.exp(-0.5 * square) * lax.rsqrt(spread)


def frame_tables(widths_ref, ftab, scales, frames):
    shape = (2 * frames, 6 * frames)
    row = lax.broadcasted_iota(jnp.int32, shape, 0)
    col = lax.broadcasted_iota(jnp.int32, shape, 1)
    row_bin = (row >= frames).astype(jnp.int32)
    part = (col >= 2 * frames).astype(jnp.int32) + (col >= 4 * frames).astype(jnp.int32)
    rest = col - part * (2 * frames)
    col_bin = (rest >= frames).astype(jnp.int32)
    offset = (rest - col_bin * frames) + (part - 1) * frames - (row - row_bin * frames)
    keep = (row_bin == col_bin) & (jnp.abs(offset) <= frames)
    offset = offset.astype(jnp.float32)
    for scale in range(scales):
        spread = jnp.full(shape, widths_ref[scale].astype(jnp.float32))
        values = mexican(offset / spread, spread)
        ftab[pl.ds(scale * 2 * frames, 2 * frames), :] = jnp.where(keep, values, 0.0).astype(
            jnp.bfloat16
        )


def scan_tables(widths_ref, hats, scales, scans):
    span = hats.shape[2]

    def one(scale, carry):
        spread = jnp.full((LANES, LANES), SCAN_RATIO * widths_ref[scale].astype(jnp.float32))
        inverse = 1.0 / spread
        root = lax.rsqrt(spread)
        base = lax.broadcasted_iota(jnp.int32, (LANES, LANES), 0) - lax.broadcasted_iota(
            jnp.int32, (LANES, LANES), 1
        )
        for tile in range(span // LANES):
            offset = (base + (scans - LANES - tile * LANES)).astype(jnp.float32)
            ratio = offset * inverse
            square = ratio * ratio
            values = (1.0 - square) * jnp.exp(-0.5 * square) * root
            hats[scale, :, tile * LANES : (tile + 1) * LANES] = values.astype(jnp.bfloat16)
        return carry

    lax.fori_loop(0, scales, one, 0)


def kernel(
    rt_count,
    widths_ref,
    slab_ref,
    peak_ref,
    energy_ref,
    raw,
    block,
    ftab,
    hats,
    smooth,
    total,
    best,
    power,
    best_out,
    best_half,
    power_out,
    in_sem,
    send_sem,
    recv_sem,
    out_sem,
):
    tiles, frames, strip, _ = raw.shape
    scales, rows, scans = total.shape
    pairs = strip // 2
    twice = 2 * frames
    me = lax.axis_index("rt")
    first_bin = pl.multiple_of(lax.axis_index("scale") * strip, strip)

    loads = []
    for tile in range(tiles):
        load = pltpu.make_async_copy(
            slab_ref.at[:, pl.ds(first_bin, strip), pl.ds(tile * LANES, LANES)],
            raw.at[tile],
            in_sem.at[tile],
        )
        load.start()
        loads.append(load)

    barrier = pltpu.get_barrier_semaphore()
    has_low, has_high = me > 0, me < rt_count - 1

    @pl.when(has_low)
    def _():
        pl.semaphore_signal(barrier, inc=1, device_id={"rt": me - 1}, device_id_type=MESH)

    @pl.when(has_high)
    def _():
        pl.semaphore_signal(barrier, inc=1, device_id={"rt": me + 1}, device_id_type=MESH)

    has_both = has_low & has_high

    @pl.when(has_both)
    def _():
        pl.semaphore_wait(barrier, 2)

    @pl.when(jnp.logical_not(has_both))
    def _():
        pl.semaphore_wait(barrier, 1)

    def copies(tile):
        own = block.at[tile, :, pl.ds(twice, twice), :]
        up = pltpu.make_async_remote_copy(
            src_ref=own,
            dst_ref=block.at[tile, :, pl.ds(0, twice), :],
            send_sem=send_sem.at[0, tile],
            recv_sem=recv_sem.at[0, tile],
            device_id={"rt": me + 1},
            device_id_type=MESH,
        )
        down = pltpu.make_async_remote_copy(
            src_ref=own,
            dst_ref=block.at[tile, :, pl.ds(2 * twice, twice), :],
            send_sem=send_sem.at[1, tile],
            recv_sem=recv_sem.at[1, tile],
            device_id={"rt": me - 1},
            device_id_type=MESH,
        )
        return up, down

    flat = raw.reshape(tiles * frames * strip, LANES)
    for tile in range(tiles):
        loads[tile].wait()
        for pair in range(pairs):
            parts = [
                flat[pl.ds(tile * frames * strip + 2 * pair + half, frames, stride=strip), :]
                for half in range(2)
            ]
            block[tile, pair, twice : 2 * twice, :] = jnp.concatenate(parts, axis=0).astype(
                jnp.bfloat16
            )
        up, down = copies(tile)
        pl.when(has_high)(up.start)
        pl.when(has_low)(down.start)

    @pl.when(jnp.logical_not(has_low))
    def _():
        block[:, :, 0:twice, :] = jnp.zeros((tiles, pairs, twice, LANES), jnp.bfloat16)

    @pl.when(jnp.logical_not(has_high))
    def _():
        block[:, :, 2 * twice : 3 * twice, :] = jnp.zeros(
            (tiles, pairs, twice, LANES), jnp.bfloat16
        )

    frame_tables(widths_ref, ftab, scales, frames)
    scan_tables(widths_ref, hats, scales, scans)

    starts = list(range(0, tiles, GROUPS))
    for start in starts:
        group = list(range(start, min(start + GROUPS, tiles)))
        depth = len(group) * LANES
        for tile in group:
            up, down = copies(tile)
            pl.when(has_low)(up.wait_recv)
            pl.when(has_high)(down.wait_recv)

        def frame_step(pair, carry):
            data = jnp.concatenate([block[tile, pair] for tile in group], axis=1)
            mixed = jnp.dot(ftab[...], data, preferred_element_type=jnp.float32)
            mixed = mixed.astype(jnp.bfloat16).reshape(scales, twice, depth)
            smooth[:, pl.ds(pl.multiple_of(pair * twice, twice), twice), 0:depth] = mixed
            return carry

        lax.fori_loop(0, pairs, frame_step, 0)

        def scan_step(scale, carry):
            table = jnp.concatenate(
                [
                    hats[scale, :, scans - LANES * (tile + 1) : 2 * scans - LANES * (tile + 1)]
                    for tile in group
                ],
                axis=0,
            )
            part = jnp.dot(
                smooth[scale, :, 0:depth], table, preferred_element_type=jnp.float32
            )
            if start > 0:
                part = part + total[scale]
            if start != starts[-1]:
                total[scale] = part
            else:
                best[...] = jnp.maximum(best[...], part)
                power[...] = power[...] + part * part
            return carry

        if start == starts[-1]:
            best[...] = jnp.full(best.shape, -jnp.inf, jnp.float32)
            power[...] = jnp.zeros(power.shape, jnp.float32)
        lax.fori_loop(0, scales, scan_step, 0)

    best_flat = best_out.reshape(tiles * frames * strip, LANES)
    power_flat = power_out.reshape(tiles * frames * strip, LANES)
    stores = []
    for tile in range(tiles):
        lanes = pl.ds(tile * LANES, LANES)
        for mz in range(strip):
            where = pl.ds(tile * frames * strip + mz, frames, stride=strip)
            best_flat[where, :] = best[mz * frames : (mz + 1) * frames, lanes]
            power_flat[where, :] = power[mz * frames : (mz + 1) * frames, lanes]
        best_half[tile] = best_out[tile].astype(jnp.bfloat16)
        for slot, (source, target) in enumerate(((best_half, peak_ref), (power_out, energy_ref))):
            store = pltpu.make_async_copy(
                source.at[tile], target.at[:, :, lanes], out_sem.at[slot, tile]
            )
            store.start()
            stores.append(store)
    for tile in range(tiles):
        up, down = copies(tile)
        pl.when(has_high)(up.wait_send)
        pl.when(has_low)(down.wait_send)
    for store in stores:
        store.wait()


def per_device(slab, widths):
    frames, mz_bins, scans = slab.shape
    scales = widths.shape[0]
    strip = mz_bins // lax.axis_size("scale")
    tiles = scans // LANES
    rows = frames * strip
    bf16, f32 = jnp.bfloat16, jnp.float32
    flops = 2 * scales * rows * scans * (scans + 6 * frames)
    return pl.pallas_call(
        functools.partial(kernel, lax.axis_size("rt")),
        out_shape=(
            jax.ShapeDtypeStruct((frames, strip, scans), bf16),
            jax.ShapeDtypeStruct((frames, strip, scans), f32),
        ),
        in_specs=[
            pl.BlockSpec(memory_space=pltpu.SMEM),
            pl.BlockSpec(memory_space=pl.ANY),
        ],
        out_specs=(pl.BlockSpec(memory_space=pl.ANY), pl.BlockSpec(memory_space=pl.ANY)),
        scratch_shapes=[
            pltpu.VMEM((tiles, frames, strip, LANES), f32),
            pltpu.VMEM((tiles, strip // 2, 6 * frames, LANES), bf16),
            pltpu.VMEM((scales * 2 * frames, 6 * frames), bf16),
            pltpu.VMEM((scales, LANES, 2 * scans - LANES), bf16),
            pltpu.VMEM((scales, rows, GROUPS * LANES), bf16),
            pltpu.VMEM((scales, rows, scans), f32),
            pltpu.VMEM((rows, scans), f32),
            pltpu.VMEM((rows, scans), f32),
            pltpu.VMEM((tiles, frames, strip, LANES), f32),
            pltpu.VMEM((tiles, frames, strip, LANES), bf16),
            pltpu.VMEM((tiles, frames, strip, LANES), f32),
            pltpu.SemaphoreType.DMA((tiles,)),
            pltpu.SemaphoreType.DMA((2, tiles)),
            pltpu.SemaphoreType.DMA((2, tiles)),
            pltpu.SemaphoreType.DMA((2, tiles)),
        ],
        compiler_params=pltpu.CompilerParams(
            collective_id=0, has_side_effects=True, vmem_limit_bytes=58 * 1024 * 1024
        ),
        cost_estimate=pl.CostEstimate(
            flops=flops, bytes_accessed=10 * rows * scans, transcendentals=0
        ),
        name="wavelets",
    )(widths, slab)


def solution(mesh):
    in_specs = (P("rt", None, None), P())
    out_specs = (P("rt", "scale", None), P("rt", "scale", None))
    return jax.shard_map(
        per_device, mesh=mesh, in_specs=in_specs, out_specs=out_specs, check_vma=False
    )
```

time: 257 us -> 36.1 us (0.14)
  waiting for transfers between devices: 107 us -> 0 us
  blocking collectives: 66.8 us -> 0 us
  local copies, waits for them, and re-layouts: 44.1 us -> 3.19 us
  Pallas kernels: 0 us -> 32.1 us
  matrix products: 17.9 us -> 0 us
  other arithmetic: 9.47 us -> 0 us
  starting transfers between devices: 9.23 us -> 0 us
    ppermute x2 -> x0, waiting for transfers between devices: 107 us -> none  [the longest x1 107 us: padded_2(): lax.ppermute(lax.slice_in_dim(block, 0, width, axis=dim), axis, backward)]
    all_to_all x1 -> x0, blocking collectives: 66.8 us -> none  [per_device(): lax.all_to_all(stacked, 'scale', split_axis=2, concat_axis=0, tiled=True)]
    pallas_call x0 -> x1, Pallas kernels: none -> 32.1 us  [per_device(): pl.pallas_call(functools.partial(kernel, lax.axis_size('rt')), out_shape=...]
    unnamed x7 -> x4, local copies, waits for them, and re-layouts: 24.4 us -> 3.19 us
    dot_general x2 -> x0, matrix products: 17.9 us -> none  [the longest x1 9.05 us: per_device(): jnp.dot(signal, scan_table, preferred_element_type=jnp.float32)]
    ppermute x2 -> x0, starting transfers between devices: 9.23 us -> none  [the longest x1 7.95 us: padded_2(): lax.ppermute(lax.slice_in_dim(block, block.shape[dim] - width, None, axis...]
    reshape x1 -> x0, local copies, waits for them, and re-layouts: 8.02 us -> none  [per_device(): smooth = smooth.reshape(frame_rows, mz_bins, scan_count)]
    concatenate x1 -> x0, local copies, waits for them, and re-layouts: 7.23 us -> none  [padded_2(): block = jnp.concatenate([low, block, high], axis=dim)]
  transfers between devices with their start and end apart: 2 -> 0, of which waited for: 1 -> 0; matrix products, arithmetic and copies ran while one was open for 6% -> 0% of each run, Pallas kernels for 0% -> 0%
where the time goes in v1:
time: 36.1 us; the launch traced here: 35.9 us
  Pallas kernels  32.1 us (89%)
  local copies, waits for them, and re-layouts  3.19 us (9%)
  between operations  0.65 us (2%)
    pallas_call x1, Pallas kernels, per_device(): pl.pallas_call(functools.partial(kernel, lax.axis_size('rt')), out_shape=...  32.1 us
    unnamed x4, local copies, waits for them, and re-layouts  3.19 us

profile of v1, /device:TPU:0, one launch (start us, length us, event | category | flops | bytes accessed | tf_op | source)
XLA Modules:
  0.0 35.9 jit_solution(16394937532476538342)
XLA Ops:
  0.6 32.1 %wavelets.1 = (bf16[24,16,896]{2,1,0:T(8,128)(2,1)}, f32[24,16,896]{2,1,0:T(8,128)}) custom-call(s32[8]{0:T(128)} %widths_ref.1, f32[24,128,896]{2,1,0:T(8,128)} %slab_ref.1), custom_call_target="tpu_custom_call" | custom-call | flops 5725224960 | bytes 3440640 | tf_op jit(solution)/shard_map/wavelets/pallas_call | solution.py:244
  32.7 0.0 copy-start
  32.7 2.1 %copy.6 = bf16[24,16,896]{2,1,0:T(8,128)(2,1)} copy(bf16[24,16,896]{2,1,0:T(8,128)(2,1)} %get-tuple-element.4) | data formatting | bytes 1376256
  34.8 0.0 copy-done
  34.8 1.1 %copy.7 = f32[24,16,896]{2,1,0:T(8,128)} copy(f32[24,16,896]{2,1,0:T(8,128)S(1)} %copy-done) | data formatting | bytes 2752512
Async XLA Ops:
  32.7 2.1 %copy-start = (f32[24,16,896]{2,1,0:T(8,128)S(1)}, f32[24,16,896]{2,1,0:T(8,128)}, u32[]{:S(2)}) copy-start(f32[24,16,896]{2,1,0:T(8,128)} %get-tuple-element.5) | copy-start | bytes 4128772

commit v2 on v1

--- a/solution.py
+++ b/solution.py
@@ -9,7 +9,11 @@
 
 SCAN_RATIO = 16
 LANES = 128
-GROUPS = 2
+EDGES = (4,)
+COLUMNS = 256
+FRAME_UNROLL = 8
+LEAD = 4
+SCAN_UNROLL = 8
 MESH = pl.DeviceIdType.MESH
 
 
@@ -138,6 +142,11 @@
         )
         return up, down
 
+    def send(tile):
+        up, down = copies(tile)
+        pl.when(has_high)(up.start)
+        pl.when(has_low)(down.start)
+
     flat = raw.reshape(tiles * frames * strip, LANES)
     for tile in range(tiles):
         loads[tile].wait()
@@ -149,9 +158,8 @@
             block[tile, pair, twice : 2 * twice, :] = jnp.concatenate(parts, axis=0).astype(
                 jnp.bfloat16
             )
-        up, down = copies(tile)
-        pl.when(has_high)(up.start)
-        pl.when(has_low)(down.start)
+        if tile < LEAD:
+            send(tile)
 
     @pl.when(jnp.logical_not(has_low))
     def _():
@@ -165,54 +173,12 @@
 
     frame_tables(widths_ref, ftab, scales, frames)
     scan_tables(widths_ref, hats, scales, scans)
-
-    starts = list(range(0, tiles, GROUPS))
-    for start in starts:
-        group = list(range(start, min(start + GROUPS, tiles)))
-        depth = len(group) * LANES
-        for tile in group:
-            up, down = copies(tile)
-            pl.when(has_low)(up.wait_recv)
-            pl.when(has_high)(down.wait_recv)
-
-        def frame_step(pair, carry):
-            data = jnp.concatenate([block[tile, pair] for tile in group], axis=1)
-            mixed = jnp.dot(ftab[...], data, preferred_element_type=jnp.float32)
-            mixed = mixed.astype(jnp.bfloat16).reshape(scales, twice, depth)
-            smooth[:, pl.ds(pl.multiple_of(pair * twice, twice), twice), 0:depth] = mixed
-            return carry
-
-        lax.fori_loop(0, pairs, frame_step, 0)
-
-        def scan_step(scale, carry):
-            table = jnp.concatenate(
-                [
-                    hats[scale, :, scans - LANES * (tile + 1) : 2 * scans - LANES * (tile + 1)]
-                    for tile in group
-                ],
-                axis=0,
-            )
-            part = jnp.dot(
-                smooth[scale, :, 0:depth], table, preferred_element_type=jnp.float32
-            )
-            if start > 0:
-                part = part + total[scale]
-            if start != starts[-1]:
-                total[scale] = part
-            else:
-                best[...] = jnp.maximum(best[...], part)
-                power[...] = power[...] + part * part
-            return carry
-
-        if start == starts[-1]:
-            best[...] = jnp.full(best.shape, -jnp.inf, jnp.float32)
-            power[...] = jnp.zeros(power.shape, jnp.float32)
-        lax.fori_loop(0, scales, scan_step, 0)
 
     best_flat = best_out.reshape(tiles * frames * strip, LANES)
     power_flat = power_out.reshape(tiles * frames * strip, LANES)
     stores = []
-    for tile in range(tiles):
+
+    def finish(tile):
         lanes = pl.ds(tile * LANES, LANES)
         for mz in range(strip):
             where = pl.ds(tile * frames * strip + mz, frames, stride=strip)
@@ -225,6 +191,78 @@
             )
             store.start()
             stores.append(store)
+
+    def table(scale, group, low, high):
+        windows = [scans - LANES * (tile + 1) for tile in group]
+        return jnp.concatenate([hats[scale, :, at + low : at + high] for at in windows], axis=0)
+
+    def frame_sums(group, place):
+        width = len(group) * LANES
+        for tile in group:
+            up, down = copies(tile)
+            pl.when(has_low)(up.wait_recv)
+            pl.when(has_high)(down.wait_recv)
+            if tile + LEAD < tiles:
+                send(tile + LEAD)
+
+        def step(turn, carry):
+            for one in range(FRAME_UNROLL):
+                pair = turn * FRAME_UNROLL + one
+                data = jnp.concatenate([block[tile, pair] for tile in group], axis=1)
+                mixed = jnp.dot(ftab[...], data, preferred_element_type=jnp.float32)
+                mixed = mixed.astype(jnp.bfloat16).reshape(scales, twice, width)
+                rows_of = pl.ds(pl.multiple_of(pair * twice, twice), twice)
+                smooth[:, rows_of, place : place + width] = mixed
+            return carry
+
+        lax.fori_loop(0, pairs // FRAME_UNROLL, step, 0)
+
+    splits = [edge for edge in EDGES if edge < tiles] + [tiles]
+    columns = [(low, min(low + COLUMNS, scans)) for low in range(0, scans, COLUMNS)]
+    begin = 0
+    for end in splits:
+        group = list(range(begin, end))
+        depth = len(group) * LANES
+        for at in range(0, len(group), 2):
+            frame_sums(group[at : at + 2], at * LANES)
+        first, last = begin == 0, end == tiles
+        begin = end
+
+        def part_of(scale, low, high):
+            part = jnp.dot(
+                smooth[scale, :, 0:depth],
+                table(scale, group, low, high),
+                preferred_element_type=jnp.float32,
+            )
+            return part if first else part + total[scale, :, low:high]
+
+        if not last:
+
+            def scan_step(scale, carry):
+                for low, high in columns:
+                    total[scale, :, low:high] = part_of(scale, low, high)
+                return carry
+
+            lax.fori_loop(0, scales, scan_step, 0)
+            continue
+        for low, high in columns:
+
+            def last_step(turn, carry):
+                peak, energy = best[:, low:high], power[:, low:high]
+                for one in range(SCAN_UNROLL):
+                    part = part_of(turn * SCAN_UNROLL + one, low, high)
+                    peak = jnp.maximum(peak, part)
+                    energy = energy + part * part
+                best[:, low:high] = peak
+                power[:, low:high] = energy
+                return carry
+
+            best[:, low:high] = jnp.full((rows, high - low), -jnp.inf, jnp.float32)
+            power[:, low:high] = jnp.zeros((rows, high - low), jnp.float32)
+            lax.fori_loop(0, scales // SCAN_UNROLL, last_step, 0)
+            for tile in range(low // LANES, high // LANES):
+                finish(tile)
+
     for tile in range(tiles):
         up, down = copies(tile)
         pl.when(has_high)(up.wait_send)
@@ -240,6 +278,8 @@
     tiles = scans // LANES
     rows = frames * strip
     bf16, f32 = jnp.bfloat16, jnp.float32
+    edges = [0] + [edge for edge in EDGES if edge < tiles] + [tiles]
+    depth = LANES * max(high - low for low, high in zip(edges, edges[1:]))
     flops = 2 * scales * rows * scans * (scans + 6 * frames)
     return pl.pallas_call(
         functools.partial(kernel, lax.axis_size("rt")),
@@ -257,7 +297,7 @@
             pltpu.VMEM((tiles, strip // 2, 6 * frames, LANES), bf16),
             pltpu.VMEM((scales * 2 * frames, 6 * frames), bf16),
             pltpu.VMEM((scales, LANES, 2 * scans - LANES), bf16),
-            pltpu.VMEM((scales, rows, GROUPS * LANES), bf16),
+            pltpu.VMEM((scales, rows, depth), bf16),
             pltpu.VMEM((scales, rows, scans), f32),
             pltpu.VMEM((rows, scans), f32),
             pltpu.VMEM((rows, scans), f32),

time: 36.1 us -> 31.3 us (0.87)
  Pallas kernels: 32.1 us -> 27.3 us
    pallas_call x1, Pallas kernels: 32.1 us -> 27.3 us  [per_device(): pl.pallas_call(functools.partial(kernel, lax.axis_size('rt')), out_shape=...]
where the time goes in v2:
time: 31.3 us; the launch traced here: 31.1 us
  Pallas kernels  27.3 us (87%)
  local copies, waits for them, and re-layouts  3.19 us (10%)
  between operations  0.65 us (2%)
    pallas_call x1, Pallas kernels, per_device(): pl.pallas_call(functools.partial(kernel, lax.axis_size('rt')), out_shape=...  27.3 us
    unnamed x4, local copies, waits for them, and re-layouts  3.19 us

profile of v2, /device:TPU:0, one launch (start us, length us, event | category | flops | bytes accessed | tf_op | source)
XLA Modules:
  0.0 31.1 jit_solution(2392402501598941831)
XLA Ops:
  0.6 27.3 %wavelets.1 = (bf16[24,16,896]{2,1,0:T(8,128)(2,1)}, f32[24,16,896]{2,1,0:T(8,128)}) custom-call(s32[8]{0:T(128)} %widths_ref.1, f32[24,128,896]{2,1,0:T(8,128)} %slab_ref.1), custom_call_target="tpu_custom_call" | custom-call | flops 5725224960 | bytes 3440640 | tf_op jit(solution)/shard_map/wavelets/pallas_call | solution.py:284
  27.9 0.0 copy-start
  27.9 2.1 %copy.6 = bf16[24,16,896]{2,1,0:T(8,128)(2,1)} copy(bf16[24,16,896]{2,1,0:T(8,128)(2,1)} %get-tuple-element.4) | data formatting | bytes 1376256
  30.0 0.0 copy-done
  30.0 1.1 %copy.7 = f32[24,16,896]{2,1,0:T(8,128)} copy(f32[24,16,896]{2,1,0:T(8,128)S(1)} %copy-done) | data formatting | bytes 2752512
Async XLA Ops:
  27.9 2.1 %copy-start = (f32[24,16,896]{2,1,0:T(8,128)S(1)}, f32[24,16,896]{2,1,0:T(8,128)}, u32[]{:S(2)}) copy-start(f32[24,16,896]{2,1,0:T(8,128)} %get-tuple-element.5) | copy-start | bytes 4128772

commit v3 on v2

--- a/solution.py
+++ b/solution.py
@@ -238,12 +238,13 @@
 
         if not last:
 
-            def scan_step(scale, carry):
-                for low, high in columns:
-                    total[scale, :, low:high] = part_of(scale, low, high)
+            def scan_step(turn, carry):
+                for scale in (turn * 2 + one for one in range(2)):
+                    for low, high in columns:
+                        total[scale, :, low:high] = part_of(scale, low, high)
                 return carry
 
-            lax.fori_loop(0, scales, scan_step, 0)
+            lax.fori_loop(0, scales // 2, scan_step, 0)
             continue
         for low, high in columns:
 

time: 31.3 us -> 30.8 us (0.984)
  Pallas kernels: 27.3 us -> 26.8 us
    pallas_call x1, Pallas kernels: 27.3 us -> 26.8 us  [per_device(): pl.pallas_call(functools.partial(kernel, lax.axis_size('rt')), out_shape=...]
where the time goes in v3:
time: 30.8 us; the launch traced here: 30.6 us
  Pallas kernels  26.8 us (87%)
  local copies, waits for them, and re-layouts  3.19 us (10%)
  between operations  0.65 us (2%)
    pallas_call x1, Pallas kernels, per_device(): pl.pallas_call(functools.partial(kernel, lax.axis_size('rt')), out_shape=...  26.8 us
    unnamed x4, local copies, waits for them, and re-layouts  3.19 us

profile of v3, /device:TPU:0, one launch (start us, length us, event | category | flops | bytes accessed | tf_op | source)
XLA Modules:
  0.0 30.6 jit_solution(2695208825369184039)
XLA Ops:
  0.6 26.8 %wavelets.1 = (bf16[24,16,896]{2,1,0:T(8,128)(2,1)}, f32[24,16,896]{2,1,0:T(8,128)}) custom-call(s32[8]{0:T(128)} %widths_ref.1, f32[24,128,896]{2,1,0:T(8,128)} %slab_ref.1), custom_call_target="tpu_custom_call" | custom-call | flops 5725224960 | bytes 3440640 | tf_op jit(solution)/shard_map/wavelets/pallas_call | solution.py:285
  27.4 0.0 copy-start
  27.4 2.1 %copy.6 = bf16[24,16,896]{2,1,0:T(8,128)(2,1)} copy(bf16[24,16,896]{2,1,0:T(8,128)(2,1)} %get-tuple-element.4) | data formatting | bytes 1376256
  29.5 0.0 copy-done
  29.5 1.1 %copy.7 = f32[24,16,896]{2,1,0:T(8,128)} copy(f32[24,16,896]{2,1,0:T(8,128)S(1)} %copy-done) | data formatting | bytes 2752512
Async XLA Ops:
  27.4 2.1 %copy-start = (f32[24,16,896]{2,1,0:T(8,128)S(1)}, f32[24,16,896]{2,1,0:T(8,128)}, u32[]{:S(2)}) copy-start(f32[24,16,896]{2,1,0:T(8,128)} %get-tuple-element.5) | copy-start | bytes 4128772
